TPU v7x, 32 devices: a whole 2x2x4 slice. The times are simulated.
32 devices in a mesh: dp: 8 (over z, core), tensor: 4 (over y, x).
Axes of the slice: x: 2, y: 2, z: 4, core: 2. Of those that a mesh axis runs over, the one named last changes fastest.
Arguments:
- inputs: float32 [8192, 1024], P(('dp', 'tensor')), may hold values from -6 to 6
- teacher: float32 [8192, 1024], P(('dp', 'tensor')), may hold values from -6 to 6
- valid_mask: int32 [8, 1024], P('dp'), may hold values from 0 to 1, as said below
- documents: int32 [8, 1024], P('dp'), may hold values from 0 to 3, never falling along the last dimension, each value on 1 to 512 neighbouring positions
- picture_starts: int32 [8, 2], P('dp'), may hold values from 0 to 768, as said below
- w_query: bfloat16 [1024, 1024], P('dp', 'tensor'), may hold values from -0.25 to 0.25
- w_key: bfloat16 [1024, 1024], P('dp', 'tensor'), may hold values from -0.25 to 0.25
- w_value: bfloat16 [1024, 1024], P('dp', 'tensor'), may hold values from -0.1875 to 0.1875
- w_out: bfloat16 [1024, 1024], P('tensor', 'dp'), may hold values from -0.75 to 0.75
- w_gate: bfloat16 [1024, 2816], P('dp', 'tensor'), may hold values from -0.1875 to 0.1875
- w_up: bfloat16 [1024, 2816], P('dp', 'tensor'), may hold values from -0.1875 to 0.1875
- w_down: bfloat16 [2816, 1024], P('tensor', 'dp'), may hold values from -0.109375 to 0.109375
Outputs:
- output: float32 [8192, 1024], P(('dp', 'tensor'))
- loss_value: float32 [], replicated
- grad_inputs: float32 [8192, 1024], P(('dp', 'tensor'))
- grad_query: float32 [1024, 1024], P('dp', 'tensor')
- grad_key: float32 [1024, 1024], P('dp', 'tensor')
- grad_value: float32 [1024, 1024], P('dp', 'tensor')
- grad_out: float32 [1024, 1024], P('tensor', 'dp')
- grad_gate: float32 [1024, 2816], P('dp', 'tensor')
- grad_up: float32 [1024, 2816], P('dp', 'tensor')
- grad_down: float32 [2816, 1024], P('tensor', 'dp')
Inputs may be any that keep to these rules, and one draw needn't show every extreme that they name: `valid_mask`: position 0 of every sequence is valid. `documents`: ids never fall along a sequence; each document has 1 to 512 tokens. `picture_starts`: piece p of a sequence starts between p * 512 and p * 512 + 1024 / 2 - 256, so the pieces of a sequence never intersect.
All inputs are finite; a program needn't handle non-finite values.
Results may differ from a plain program's by a relative error of at most 0.017.
Values may be sent and summed in bfloat16 or wider, within the bound.
A program may use at most 128 MiB of HBM per device.

v0:
```python
import functools

import jax
import jax.numpy as jnp
import numpy as np
from jax import lax
from jax.experimental import pallas as pl
from jax.experimental.pallas import tpu as pltpu
from jax.sharding import PartitionSpec as P

MESH = pl.DeviceIdType.MESH
HD = 64
PIECE = 256
EPS = 1e-5
MASKED = -1e30
VMEM_BYTES = 60 * 2**20
BF = jnp.bfloat16
F32 = jnp.float32
NT = (((1,), (1,)), ((), ()))
NN = (((1,), (0,)), ((), ()))


def dot(a, b, dims=NN):
    return lax.dot_general(a, b, dims, preferred_element_type=F32)


def eye(n):
    return (
        lax.broadcasted_iota(jnp.int32, (n, n), 0) == lax.broadcasted_iota(jnp.int32, (n, n), 1)
    ).astype(F32).astype(BF)


def turned(a):
    n = a.shape[1]
    step = min(n, 256)
    parts = [dot(eye(step), a[:, k : k + step], NT).astype(BF) for k in range(0, n, step)]
    return parts[0] if len(parts) == 1 else jnp.concatenate(parts, axis=0)


def mean_of(v):
    return jnp.sum(v, axis=1, keepdims=True) * (1.0 / v.shape[1])


def normed(v):
    centred = v - mean_of(v)
    inv = lax.rsqrt(mean_of(centred * centred) + EPS)
    return centred * inv, inv


def normed_back(n, inv, g):
    return inv * (g - mean_of(g) - n * mean_of(g * n))


class Geo:
    def __init__(self, n_dp, n_t, tok_rows, d_model, cols, hid):
        self.n_dp, self.n_t, self.R, self.D, self.c, self.f = n_dp, n_t, tok_rows, d_model, cols, hid
        self.C = n_dp // 2
        self.S = tok_rows * n_t
        self.H = cols // HD
        self.Dn = d_model // n_dp
        self.square = n_t == 4
        self.line = self.C == 4

    def place(self):
        self.d = lax.axis_index("dp")
        self.t = lax.axis_index("tensor")
        self.chip = self.d // 2
        self.core = self.d % 2
        if self.square:
            self.tx = self.t + 1 - 2 * (self.t % 2)
            self.ty = (self.t + 2) % 4
            self.td = 3 - self.t
            self.to = [self.tx, self.ty]
            self.leave = [self.td, self.tx, self.ty, self.t]
        else:
            n = self.n_t
            self.to = [(self.t + k) % n for k in range(1, n)]
            self.leave = [(self.t + k) % n for k in range(1, n)] + [self.t]
        self.sib = self.d + 1 - 2 * self.core
        return self

    def leave_at(self, i):
        if self.square:
            return 2 * ((self.t // 2 + i + 1) % 2) + (self.t % 2 + 1 - i // 2) % 2
        return (self.t + 1 + i) % self.n_t

    def arrive_at(self, i):
        if self.square:
            return 2 * ((self.t // 2 + i // 2) % 2) + (self.t % 2 + i % 2) % 2
        return (self.t + self.n_t - i) % self.n_t

    def far_at(self, i):
        if self.square:
            return 2 * ((self.t // 2 + i % 2) % 2) + (self.t % 2 + (i + 1) // 2) % 2
        return (self.t + self.n_t - i) % self.n_t

    def far_lead(self, i):
        return i - 1 if self.square else self.n_t - 1 - i

    def zto(self, k):
        return ((self.chip + k) % self.C) * 2 + self.core

    def zfrom(self, k):
        return ((self.chip + self.C - k) % self.C) * 2 + self.core

    def rows(self, blk, first=0, count=None):
        count = self.R if count is None else count
        return pl.ds(pl.multiple_of(blk * self.R + first, count), count)

    def wrows(self, d):
        return pl.ds(pl.multiple_of(d * self.Dn, self.Dn), self.Dn)

    def greet(self):
        bar = pltpu.get_barrier_semaphore()
        out = [(self.d, p) for p in self.to]
        out += [(self.zto(k), self.t) for k in range(1, self.C)] + [(self.sib, self.t)]
        for dev in out:
            pl.semaphore_signal(bar, inc=1, device_id=dev, device_id_type=MESH)
        self.met = len(out)

    def meet(self):
        pl.semaphore_wait(pltpu.get_barrier_semaphore(), self.met)


class Comm:
    def __init__(self, send_sem, recv_sem):
        self.ss, self.rs = send_sem, recv_sem
        self.n = self.groups = 0

    def slots(self, k):
        self.n += k
        return list(range(self.n - k, self.n))

    def group(self):
        self.groups += 1
        return self.groups - 1

    def _copy(self, group, slot, src, dst, dev):
        return pltpu.make_async_remote_copy(
            src_ref=src, dst_ref=dst, send_sem=self.ss.at[group], recv_sem=self.rs.at[slot], device_id=dev, device_id_type=MESH
        )

    def send(self, group, slot, src, dst, dev, when=None):
        copy = self._copy(group, slot, src, dst, dev)
        if when is None:
            copy.start()
        else:
            pl.when(when)(copy.start)

    def recv(self, slot, dst, dev, when=None):
        copy = self._copy(0, slot, dst, dst, dev)
        if when is None:
            copy.wait_recv()
        else:
            pl.when(when)(copy.wait_recv)

    def sent(self, group, like, dev, when=None):
        copy = self._copy(group, 0, like, like, dev)
        if when is None:
            copy.wait_send()
        else:
            pl.when(when)(copy.wait_send)


class Gather:
    def __init__(self, geo, comm, slots, group, buf, far_first=False):
        self.g, self.comm, self.buf, self.group = geo, comm, buf, group
        g = geo
        self.far_first = far_first and g.square
        if not g.square:
            self.s = slots
            self.order = [(g.t + g.n_t - k) % g.n_t for k in range(g.n_t)]
            self.lead = [g.n_t - 1] + [g.n_t - 1 - k for k in range(1, g.n_t)]
            return
        self.sx, self.sy = slots[:5], slots[5:]
        if self.far_first:
            self.order, self.lead = [g.t, g.td, g.tx, g.ty], [3, 0, 1, 2]
        else:
            self.order, self.lead = [g.t, g.tx, g.ty, g.td], [3, 1, 2, 0]

    def begin(self, i):
        g, comm = self.g, self.comm
        if g.square:
            self._give(self.sx[i], g.t, i, 1, g.tx)
            self._give(self.sy[i], g.t, 2 + i, 1, g.ty)
            if i == 1 and not self.far_first:
                self._rest()
        elif i == 1:
            own = self.buf.at[g.rows(g.t)]
            for k, peer in enumerate(g.to):
                comm.send(self.group, self.s[k], own, own, (g.d, peer))

    def sent(self):
        self.comm.sent(self.group, self.buf.at[0 : (self.g.n_t - 1) * self.g.R], (self.g.d, self.g.to[0]))

    def piece(self, blk, first, count):
        q = self.g.R // 4
        rows = pl.ds(pl.multiple_of(blk * self.g.R + first * q, q), count * q)
        return self.buf.at[rows]

    def _give(self, slot, blk, first, count, to):
        part = self.piece(blk, first, count)
        self.comm.send(self.group, slot, part, part, (self.g.d, to))

    def _rest(self):
        g = self.g
        self._give(self.sx[4], g.t, 2, 2, g.tx)
        self._give(self.sy[4], g.t, 0, 2, g.ty)

    def relay(self):
        g, comm = self.g, self.comm
        if not g.square:
            return
        for i in range(2):
            comm.recv(self.sx[i], self.piece(g.tx, i, 1), (g.d, g.tx))
            self._give(self.sy[2 + i], g.tx, i, 1, g.ty)
            comm.recv(self.sy[i], self.piece(g.ty, 2 + i, 1), (g.d, g.ty))
            self._give(self.sx[2 + i], g.ty, 2 + i, 1, g.tx)
        if self.far_first:
            self._rest()

    def wait(self, i):
        g, comm = self.g, self.comm
        if i == 0:
            return
        if not g.square:
            comm.recv(self.s[i - 1], self.buf.at[g.rows(self.order[i])], (g.d, self.order[i]))
            return
        which = "dxy"[i - 1] if self.far_first else "xyd"[i - 1]
        if which == "x":
            comm.recv(self.sx[4], self.piece(g.tx, 2, 2), (g.d, g.tx))
        elif which == "y":
            comm.recv(self.sy[4], self.piece(g.ty, 0, 2), (g.d, g.ty))
        else:
            for k in range(2):
                comm.recv(self.sx[2 + k], self.piece(g.td, 2 + k, 1), (g.d, g.tx))
                comm.recv(self.sy[2 + k], self.piece(g.td, k, 1), (g.d, g.ty))


def scatter_scratch(g):
    h = g.R // 2
    if g.square:
        return [pltpu.VMEM((3, 2, h, g.D), BF), pltpu.VMEM((2, h, g.D), BF), pltpu.VMEM((2, h, g.D), BF), pltpu.VMEM((2, 2, h, g.D), BF)]
    return [pltpu.VMEM((g.n_t - 1, 2, h, g.D), BF), pltpu.VMEM((1, 16, 128), BF), pltpu.VMEM((1, 16, 128), BF), pltpu.VMEM((g.n_t - 1, 2, h, g.D), BF)]


class Scatter:
    def __init__(self, geo, comm, slots, group, bufs):
        self.g, self.comm, self.group = geo, comm, group
        self.part, self.into, self.out, self.fin = bufs
        g = geo
        if g.square:
            self.sx, self.sy = slots[:4], slots[4:]
        else:
            self.s = slots

    def give(self, i, value):
        h = self.g.R // 2
        for j in range(2):
            self.part[i, j] = value[j * h : (j + 1) * h].astype(BF)
        if isinstance(i, int):
            self.send(i)
        else:
            for k in range(self.g.n_t - 1):
                pl.when(i == k)(functools.partial(self.send, k))

    def send(self, i):
        g, comm = self.g, self.comm
        if not g.square:
            comm.send(self.group, self.s[i], self.part.at[i], self.fin.at[i], (g.d, g.leave[i]))
        elif i == 0:
            comm.send(self.group, self.sx[0], self.part.at[0, 0], self.into.at[0], (g.d, g.tx))
            comm.send(self.group, self.sy[0], self.part.at[0, 1], self.into.at[1], (g.d, g.ty))
        elif i == 1:
            comm.send(self.group, self.sx[1], self.part.at[1, 0], self.fin.at[0, 0], (g.d, g.tx))
        else:
            comm.send(self.group, self.sy[1], self.part.at[2, 1], self.fin.at[1, 1], (g.d, g.ty))

    def relay(self):
        g, comm = self.g, self.comm
        if not g.square:
            return
        q = g.R // 4
        comm.recv(self.sx[0], self.into.at[0], (g.d, g.tx))
        comm.recv(self.sy[0], self.into.at[1], (g.d, g.ty))
        for k in range(2):
            rows = slice(k * q, (k + 1) * q)
            for a, mine, slots, to in ((0, (2, 0), self.sy, g.ty), (1, (1, 1), self.sx, g.tx)):
                self.out[a, rows] = (self.into[a, rows].astype(F32) + self.part[(*mine, rows)].astype(F32)).astype(BF)
                comm.send(self.group, slots[2 + k], self.out.at[a, rows], self.fin.at[1 - a, a, rows], (g.d, to))

    def take(self, i, own):
        g, comm = self.g, self.comm
        q = g.R // 4
        count = 2 if g.square else g.n_t - 1
        inner = slice(i * q, (i + 1) * q)
        if g.square:
            if i == 0:
                comm.recv(self.sx[1], self.fin.at[0, 0], (g.d, g.tx))
                comm.recv(self.sy[1], self.fin.at[1, 1], (g.d, g.ty))
            comm.recv(self.sx[2 + i], self.fin.at[0, 1, inner], (g.d, g.tx))
            comm.recv(self.sy[2 + i], self.fin.at[1, 0, inner], (g.d, g.ty))
        elif i == 0:
            for k in range(count):
                comm.recv(self.s[k], self.fin.at[k], (g.d, (g.t + g.n_t - k - 1) % g.n_t))
        pairs = []
        for j in range(2):
            rows = slice(2 * j * q + i * q, 2 * j * q + (i + 1) * q)
            v = own[rows]
            for k in range(count):
                v = v + self.fin[k, j, inner].astype(F32)
            pairs.append((rows, v))
        if i == 1:
            comm.sent(self.group, self.part, (g.d, g.to[0]))
        return pairs


class WeightGather:
    def __init__(self, geo, comm, buf, first, n):
        self.g, self.comm, self.buf, self.of = geo, comm, buf, pl.ds(first, n)
        g = geo
        self.group = comm.group()
        self.inner = (g.chip == 1) | (g.chip == 2)
        self.sz, self.sc = comm.slots(g.C - 1), comm.slots(g.C)

    def at(self, d):
        return self.buf.at[self.of, self.g.wrows(d)]

    def far(self):
        g, comm = self.g, self.comm
        if g.line:
            comm.send(self.group, self.sz[1], self.at(g.d), self.at(g.d), (g.zto(2), g.t))

    def near(self):
        g, comm = self.g, self.comm
        own = self.at(g.d)
        for k in range(1, g.C):
            if g.line and k == 2:
                continue
            near = g.chip != (0 if k == 3 else 3) if g.line else None
            comm.send(self.group, self.sz[k - 1], own, own, (g.zto(k), g.t), when=near)
        comm.send(self.group, self.sc[0], own, own, (g.sib, g.t))

    def _take(self, k, when=None):
        g, comm = self.g, self.comm
        block = self.at(g.zfrom(k))
        comm.recv(self.sz[k - 1], block, (g.zfrom(k), g.t), when=when)
        comm.send(self.group, self.sc[k], block, block, (g.sib, g.t), when=when)

    def relay(self):
        g, comm = self.g, self.comm
        if not g.line:
            return
        self._take(2, self.inner)
        block = self.at(g.zfrom(2))
        comm.send(self.group, self.sz[2], block, block, (6 + g.core, g.t), when=g.chip == 2)
        comm.send(self.group, self.sz[0], block, block, (g.core, g.t), when=g.chip == 1)

    def pass_on(self):
        g = self.g
        for k in range(1, g.C):
            self._take(k, jnp.logical_not(self.inner) if g.line and k == 2 else None)

    def wait(self):
        g, comm = self.g, self.comm
        for k in range(g.C):
            other = g.zfrom(k) + 1 - 2 * g.core
            comm.recv(self.sc[k], self.at(other), (g.sib, g.t))

    def sent(self):
        g, comm = self.g, self.comm

        def some(n, when=None):
            comm.sent(self.group, self.buf.at[self.of, 0 : n * g.Dn], (g.sib, g.t), when)

        if g.line:
            some(8, self.inner)
            some(6, jnp.logical_not(self.inner))
        else:
            some(2 * g.C - 1)


class WeightScatter:
    def __init__(self, geo, comm, src, bufs):
        self.g, self.comm, self.src = geo, comm, src
        self.sib_in, self.out, self.fin = bufs
        g = geo
        self.group = comm.group()
        self.sc, self.sz = comm.slots(1)[0], comm.slots(5 if g.line else g.C - 1)
        half = g.chip // 2
        self.near, self.inner, self.other, self.opposite = 3 * half, 1 + half, 2 - half, 3 - 3 * half
        self.end = (g.chip == 0) | (g.chip == 3)

    def start(self):
        g, comm = self.g, self.comm
        for j in range(g.C):
            block = self.src.at[g.wrows(2 * j + 1 - g.core)]
            comm.send(self.group, self.sc, block, self.sib_in.at[j], (g.sib, g.t))

    def _sum(self, chip):
        return self.src[self.g.wrows(2 * chip + self.g.core)].astype(F32) + self.sib_in[chip].astype(F32)

    def meet(self):
        g, comm = self.g, self.comm
        comm.recv(self.sc, self.sib_in, (g.sib, g.t))

    def part(self, b):
        g, comm = self.g, self.comm
        if not g.line:
            for k in range(1, g.C) if b == 0 else ():
                self.out[k - 1][...] = self._sum((g.chip + k) % g.C).astype(BF)
                comm.send(self.group, self.sz[k - 1], self.out[k - 1], self.fin.at[k - 1], (g.zto(k), g.t))
            return

        @pl.when(self.end)
        def _():
            self.out[b][...] = self._sum((self.opposite, self.other, self.inner)[b]).astype(BF)

        to = (self.inner * 2 + g.core, g.t)
        comm.send(self.group, self.sz[b], self.out[b], self.fin.at[b], to, when=self.end)

    def pass_on(self):
        self.meet()
        for b in range(3):
            self.part(b)

    def relay(self, b):
        g, comm = self.g, self.comm
        if not g.line:
            return
        middle = jnp.logical_not(self.end)
        came = (0, 1, 3)[b]

        @pl.when(middle)
        def _():
            comm.recv(self.sz[came], self.fin.at[came], (g.sib, g.t))
            mine = self._sum((self.opposite, self.other, self.near)[b])
            self.out[b][...] = (mine + self.fin[came].astype(F32)).astype(BF)

        goes = (3, 4, 0)[b]
        to = ((self.other, self.other, self.near)[b] * 2 + g.core, g.t)
        comm.send(self.group, self.sz[goes], self.out[b], self.fin.at[goes], to, when=middle)

    def sent(self):
        g = self.g
        self.comm.sent(self.group, self.src.at[0 : (2 * g.C - 1) * g.Dn], (g.sib, g.t))

    def total(self):
        g, comm = self.g, self.comm
        mine = self.src[g.wrows(g.d)].astype(F32) + self.sib_in[g.chip].astype(F32)
        if not g.line:
            for k in range(1, g.C):
                comm.recv(self.sz[k - 1], self.fin.at[k - 1], (g.zfrom(k), g.t))
                mine = mine + self.fin[k - 1].astype(F32)
            return mine
        middle = jnp.logical_not(self.end)
        comm.recv(self.sz[0], self.fin.at[0], (g.sib, g.t), when=self.end)
        comm.recv(self.sz[2], self.fin.at[2], (g.sib, g.t), when=middle)
        comm.recv(self.sz[4], self.fin.at[4], (g.sib, g.t), when=middle)
        at_end = self.fin[0].astype(F32)
        between = self.fin[2].astype(F32) + self.fin[4].astype(F32)
        return mine + jnp.where(self.end, at_end, between)


def weight_scatter_scratch(g, n, w):
    steps = 5 if g.line else g.C - 1
    return [pltpu.VMEM((n, g.C, g.Dn, w), BF), pltpu.VMEM((n, g.C - 1, g.Dn, w), BF), pltpu.VMEM((n, steps, g.Dn, w), BF)]


def rotated(v, cosine, sine):
    n = v.shape[1]
    if n > cosine.shape[1]:
        cosine = jnp.concatenate([cosine] * (n // cosine.shape[1]), axis=1)
        sine = jnp.concatenate([sine] * (n // sine.shape[1]), axis=1)
    lower = lax.broadcasted_iota(jnp.int32, v.shape, 1) % HD < HD // 2
    swapped = jnp.where(lower, pltpu.roll(v, n - HD // 2, 1), pltpu.roll(v, HD // 2, 1))
    return v * cosine + swapped * sine


def head_lanes(v, h):
    lane = lax.broadcasted_iota(jnp.int32, v.shape, 1)
    keep = (lane >= h * HD) & (lane < (h + 1) * HD)
    return jnp.where(keep, v, jnp.zeros_like(v))


def attend(g, hi, q_blk, keys_rot, values_t, bias, probs, inverse):
    H, R = g.H, g.R
    step = min(512, hi)
    spans = [slice(k, k + step) for k in range(0, hi, step)]
    scores, top, sums, mix = {}, [None] * H, [None] * H, [None] * H

    def fold(v, op):
        return op(v.reshape(v.shape[0] // 8, 8, v.shape[1]), axis=0)

    def first(h, span):
        s = dot(keys_rot[span], head_lanes(q_blk, h), NT) + bias[span]
        scores[h, span.start] = s
        most = fold(s, jnp.max)
        top[h] = most if top[h] is None else jnp.maximum(top[h], most)

    def second(h, span):
        if span.start == 0:
            top[h] = jnp.max(top[h], axis=0, keepdims=True)
        e = jnp.exp(scores.pop((h, span.start)) - top[h])
        some = fold(e, jnp.sum)
        sums[h] = some if sums[h] is None else sums[h] + some
        low = e.astype(BF)
        probs[span, h * R : (h + 1) * R] = low
        out = dot(values_t[h * HD : (h + 1) * HD, span], low)
        mix[h] = out if mix[h] is None else mix[h] + out

    for h in range(H + 1):
        for span in spans:
            if h < H:
                first(h, span)
            if h > 0:
                second(h - 1, span)
    for h in range(H):
        inv = 1.0 / jnp.sum(sums[h], axis=0, keepdims=True)
        inverse[h : h + 1, :] = inv
        mix[h] = mix[h] * inv
    return jnp.concatenate(mix, axis=0)


def attend_back(g, hi, values, keys_t, probs, go, qm, dots, dk, dv):
    H, R = g.H, g.R
    step = 256 if hi < g.S else hi
    grads = [None] * H
    for k in range(0, hi + step, step):
        now, past = slice(k, k + step), slice(k - step, k)
        if k < hi:
            if step < hi:
                dv[now] += dot(probs[now], go[...])
            ahead = [dot(values[now], go[0:R], NT)]
            for h in range(H):
                cols = slice(h * R, (h + 1) * R)
                if h + 1 < H:
                    ahead.append(dot(values[now], go[(h + 1) * R : (h + 2) * R], NT))
                low = (probs[now, cols].astype(F32) * (ahead[h] - dots[h])).astype(BF)
                if h == 0 and step == hi:
                    dv[now] += dot(probs[now], go[...])
                probs[now, cols] = low
                out = dot(keys_t[h * HD : (h + 1) * HD, now], low)
                grads[h] = out if grads[h] is None else grads[h] + out
        if k > 0:
            dk[past] += dot(probs[past], qm[...])
    return jnp.concatenate(grads, axis=0)


def bias_of(qinfo, kinfo, first, size, rows):
    shape = (size, rows)
    doc_q, pic_q = qinfo[0:1, :], qinfo[1:2, :]
    key_doc, pic_k = kinfo[:, 0:1], kinfo[:, 1:2]
    key_pos = lax.broadcasted_iota(jnp.int32, shape, 0)
    query_pos = lax.broadcasted_iota(jnp.int32, shape, 1) + first
    before = key_pos <= query_pos
    open_ = (doc_q == key_doc) & (before | (pic_q == pic_k))
    ok = open_ | (key_pos == query_pos)
    return jnp.where(ok, 0.0, MASKED).astype(F32)


def rotary(length, cols):
    half = HD // 2
    frequency = 10000.0 ** (-2.0 * np.arange(half) / HD)
    angle = np.arange(length)[:, None] * frequency[None, :]
    cosine = np.concatenate([np.cos(angle)] * 2, axis=1)
    sine = np.concatenate([-np.sin(angle), np.sin(angle)], axis=1)
    reps = max(1, min(cols, 128) // HD)
    return (jnp.asarray(np.tile(cosine, (1, reps)), F32), jnp.asarray(np.tile(sine, (1, reps)), F32))


def in_slot(g, n_pic, blk):
    per = g.n_t // n_pic

    def run(body):
        for p in range(n_pic):
            pl.when(blk // per == p)(functools.partial(body, p, blk - p * per, (p + 1) * (g.S // n_pic)))

    return run


def layer_body(g, n_pic, x, teacher, valid_mask, documents, starts, wq, wk, wv, wo, wg, wu, wd, cosine, sine,
               o_out, o_in, o_q, o_k, o_v, o_o, o_g, o_u, o_d, o_loss,
               rows1, rows2, gm, ga, wa, wm, qkv, mixed, mixt, turn, wo_t, probs0, probs1, acc2, qm, gom, mids, middle, cot,
               qinfo, kinfo, rinv, cnt, err,
               part, into, out, fin,
               sib_m, fin_m, sib_a, out_a, fin_a, output, grad_inputs, dattn, dout, dmlp, stats,
               ts, tr, zs, zr, local):
    g.place()
    g.greet()
    R, S, c, H, C, Dn = g.R, g.S, g.c, g.H, g.C, g.Dn
    tc, zc = Comm(ts, tr), Comm(zs, zr)
    sums = (part, into, out, fin)
    few, ag_group, rs_group = tc.group(), tc.group(), tc.group()
    ag_slots = tc.slots(10 if g.square else g.n_t - 1)
    rs_slots = tc.slots(8 if g.square else g.n_t - 1)
    te = tc.slots(2 if g.square else g.n_t - 1)
    gather = functools.partial(Gather, g, tc, ag_slots, ag_group)
    scatter = functools.partial(Scatter, g, tc, rs_slots, rs_group, sums)
    q, kk, v = qkv.at[0], qkv.at[1], qkv.at[2]
    probs = (probs0, probs1)
    bias, dk, dv = acc2.at[:, :, :R], acc2.at[0, :, :c], acc2.at[1, :, :c]
    stores = []

    def store(buf, to):
        copy = pltpu.make_async_copy(buf, to, local.at[1 + len(stores)])
        copy.start()
        stores.append(copy)

    get_teacher = pltpu.make_async_copy(teacher, cot, local.at[0])
    get_teacher.start()

    one, _ = normed(x[...])
    rows1[g.rows(g.t)] = one.astype(BF)
    block = g.wrows(g.d)
    wa[0, block] = wq[...]
    wa[1, block] = wk[...]
    wa[2, block] = wv[...]
    g.meet()
    ag = gather(rows1)
    ag.begin(0)
    ag.begin(1)
    za, zo = WeightGather(g, zc, wa, 0, 3), WeightGather(g, zc, wa, 3, 1)
    zg, zd = WeightGather(g, zc, wm, 0, 2), WeightGather(g, zc, wm, 2, 1)
    za.far()
    wa[3, block] = turned(wo[...])
    zo.far()
    za.near()
    wm[0, block] = turned(wg[...])
    wm[1, block] = turned(wu[...])
    wm[2, block] = turned(wd[...])

    csib, cz = zc.slots(1)[0], zc.slots(C - 1)
    gsib, gz = zc.group(), zc.group()
    valid, doc = valid_mask[...], documents[...]
    cnt[0] = jnp.broadcast_to(jnp.sum(valid.astype(F32), axis=1, keepdims=True), (8, 128))
    zc.send(gsib, csib, cnt.at[0], cnt.at[1], (g.sib, g.t))
    at = lax.broadcasted_iota(jnp.int32, (1, S), 1)
    pic = jnp.zeros((1, S), jnp.int32)
    for p in range(n_pic):
        first = starts[0:1, p : p + 1]
        pic = jnp.where((at >= first) & (at < first + PIECE), p + 1, pic)
    qinfo[0:1] = doc
    qinfo[1:2] = pic
    as_keys = [jnp.where(valid == 1, doc, -1), jnp.where(pic > 0, pic, -1), valid]
    as_keys = jnp.concatenate([a.astype(F32) for a in as_keys] + [jnp.zeros((125, S), F32)], axis=0)
    kinfo[...] = as_keys.T.astype(jnp.int32)
    zc.recv(csib, cnt.at[1], (g.sib, g.t))
    cnt[2] = cnt[0] + cnt[1]
    for k in range(1, C):
        zc.send(gz, cz[k - 1], cnt.at[2], cnt.at[2 + k], (g.zto(k), g.t))

    def set_bias(i, blk):
        @in_slot(g, n_pic, blk)
        def _(p, index, hi):
            bias[i % 2, 0:hi] = bias_of(qinfo[:, g.rows(blk)], kinfo[0:hi], blk * R, hi, R)

    set_bias(0, g.leave[0])

    ag.relay()
    za.relay()
    zo.relay()
    zo.near()
    za.pass_on()
    za.wait()
    zg.far()
    zg.near()
    for i, blk in enumerate(ag.order):
        ag.wait(i)
        at = g.rows(blk)
        row = rows1[at]
        cos_b, sin_b = cosine[at], sine[at]
        q[at] = (rotated(dot(row, wa[0]), cos_b, sin_b) * HD**-0.5).astype(BF)
        kk[at] = rotated(dot(row, wa[1]), cos_b, sin_b).astype(BF)
        v[at] = dot(row, wa[2]).astype(BF)
    zo.pass_on()
    turn[...] = turned(v[...])

    rs = scatter()
    @pl.loop(0, g.n_t)
    def _(i):
        blk = g.leave_at(i)
        at = g.rows(blk)

        @pl.when(i > 0)
        def _():
            set_bias(i, blk)

        @in_slot(g, n_pic, blk)
        def _(p, index, hi):
            both = attend(g, hi, q[at], kk, turn, bias.at[i % 2], probs[p].at[index], rinv.at[blk])
            mixt[blk] = both.astype(BF)
            mixed[at] = both.T.astype(BF)

        pl.when(i == 0)(zo.wait)

        @pl.when(i == 2)
        def _():
            zg.relay()
            zd.far()
            zd.near()

        @pl.when(i < g.n_t - 1)
        def _():
            rs.give(i, dot(mixed[at], wa[3], NT))

    rs.relay()
    middle[0:R] = x[...] + dot(mixed[g.rows(g.t)], wa[3], NT)
    ag.sent()
    ag = gather(rows2, far_first=True)

    for i in range(2):
        for rows, summed in rs.take(i, middle):
            middle[rows] = summed
            two, _ = normed(summed)
            rows2[g.rows(g.t, rows.start, R // 4)] = two.astype(BF)
        ag.begin(i)
    rs = scatter()
    zd.relay()
    ag.relay()
    zg.pass_on()
    zg.wait()

    @pl.loop(0, g.n_t)
    def _(i):
        for k in range(1, g.n_t):
            pl.when(i == k)(functools.partial(ag.wait, k))
        at = g.rows(g.far_at(i))
        row = rows2[at]
        gate, up = dot(row, wm[0]), dot(row, wm[1])
        sig = jax.nn.sigmoid(gate)
        act = gate * sig
        mids[0, at] = (act * up).astype(BF)
        mids[2, at] = act.astype(BF)
        mids[1, at] = (up * sig * (1.0 + gate * (1.0 - sig))).astype(BF)

        @pl.when(i == 1)
        def _():
            zd.pass_on()
            zd.wait()

        @pl.when(i > 0)
        def _():
            rs.give(g.far_lead(i), dot(mids[0, at], wm[2], NT))

    output[...] = middle[0:R] + dot(mids[0, g.rows(g.t)], wm[2], NT)
    wo_t[...] = turned(wa[3])
    rs.relay()

    get_teacher.wait()
    tokens = cnt[2]
    for k in range(1, C):
        zc.recv(cz[k - 1], cnt.at[2 + k], (g.zfrom(k), g.t))
        tokens = tokens + cnt[2 + k]
    share = 1.0 * S * g.n_dp / tokens[0:1, 0:1]
    ag.sent()
    ag = gather(gm, far_first=True)
    errors = jnp.zeros((R // 4, 1), F32)
    for i in range(2):
        for rows, summed in rs.take(i, output):
            output[rows] = summed
            dev = summed - cot[rows]
            kept = kinfo[g.rows(g.t, rows.start, R // 4), 2:3].astype(F32) * dev
            cotangent = kept * share
            cot[rows] = cotangent
            gm[g.rows(g.t, rows.start, R // 4)] = cotangent.astype(BF)
            errors += jnp.sum(kept * dev, axis=1, keepdims=True)
        ag.begin(i)
    store(output, o_out)
    err[0] = jnp.broadcast_to(jnp.sum(errors, axis=0, keepdims=True), (8, 128))

    rs = scatter()
    if g.square:
        tc.send(few, te[0], err.at[0], err.at[1], (g.d, g.tx))
    else:
        for k, peer in enumerate(g.to):
            tc.send(few, te[k], err.at[0], err.at[1 + k], (g.d, peer))

    @pl.loop(0, g.n_t)
    def _(i):
        for k in range(1, g.n_t):
            pl.when(i == k)(functools.partial(ag.wait, k))
        at = g.rows(g.far_at(i))
        gh = dot(gm[at], wm[2])
        mids[1, at] = (gh * mids[1, at].astype(F32)).astype(BF)
        mids[2, at] = (gh * mids[2, at].astype(F32)).astype(BF)

        @pl.when(i == 0)
        def _():
            ag.relay()
            rows2[...] = turned(rows2[...])
            turn[...] = turned(kk[...])

        @pl.when(i > 0)
        def _():
            rs.give(g.far_lead(i), dot(mids[1, at], wm[0], NT) + dot(mids[2, at], wm[1], NT))

    at = g.rows(g.t)
    grad_inputs[...] = dot(mids[1, at], wm[0], NT) + dot(mids[2, at], wm[1], NT)
    zg.sent()
    zd.sent()
    wm[0] = dot(rows2[...], mids[1]).astype(BF)

    zscat = []

    def start_mlp(j, used):
        spare = [mids.at[used, k * Dn : (k + 1) * Dn] for k in range(C - 1)]
        zscat.append(WeightScatter(g, zc, wm.at[j], (sib_m.at[j], spare, fin_m.at[j])))
        zscat[-1].start()

    start_mlp(0, 1)
    rs.relay()
    zscat[0].pass_on()
    wm[1] = dot(rows2[...], mids[2]).astype(BF)
    start_mlp(1, 2)
    for k in range(0, g.D, 256):
        wm[2, k : k + 256] = dot(turned(gm[:, k : k + 256]), mids[0]).astype(BF)
    start_mlp(2, 0)
    zscat[1].pass_on()
    two, inv = normed(middle[0:R])
    ag.sent()
    ag = gather(ga)
    for i in range(2):
        for rows, back in rs.take(i, grad_inputs):
            grad_middle = cot[rows] + normed_back(two[rows], inv[rows], back)
            cot[rows] = grad_middle
            ga[g.rows(g.t, rows.start, R // 4)] = grad_middle.astype(BF)
        ag.begin(i)

    for j in (3, 0, 1, 2):
        spare = [out_a.at[j, k] for k in range(C - 1)]
        zscat.append(WeightScatter(g, zc, wa.at[j], (sib_a.at[j], spare, fin_a.at[j])))

    rs = scatter()
    zscat[2].pass_on()
    zscat[0].relay(0)
    zscat[0].relay(1)
    base = 4 if g.square else g.n_t
    ec, ez = zc.slots(1)[0], zc.slots(C - 1)
    gec, gez = zc.group(), zc.group()
    if g.square:
        tc.recv(te[0], err.at[1], (g.d, g.tx))
        err[2] = err[0] + err[1]
        tc.send(few, te[1], err.at[2], err.at[3], (g.d, g.ty))
    acc2[...] = jnp.zeros_like(acc2)
    middle[0:c] = jnp.zeros((c, g.D), F32)

    @pl.loop(0, g.n_t)
    def _(i):
        @pl.when(i == 1)
        def _():
            zscat[0].relay(2)
            rows1[...] = turned(rows1[...])
            if g.square:
                tc.recv(te[1], err.at[3], (g.d, g.ty))
                err[base] = err[2] + err[3]
            else:
                total = err[0]
                for k in range(1, g.n_t):
                    tc.recv(te[k - 1], err.at[k], (g.d, (g.t + g.n_t - k) % g.n_t))
                    total = total + err[k]
                err[base] = total
            zc.send(gec, ec, err.at[base], err.at[base + 1], (g.sib, g.t))

        @pl.when(i == 2)
        def _():
            zc.recv(ec, err.at[base + 1], (g.sib, g.t))
            err[base + 2] = err[base] + err[base + 1]
            for k in range(1, C):
                zc.send(gez, ez[k - 1], err.at[base + 2], err.at[base + 2 + k], (g.zto(k), g.t))

        for k in range(1, g.n_t):
            pl.when(i == k)(functools.partial(ag.wait, k))
        blk = g.arrive_at(i)
        at = g.rows(blk)
        middle[0:c] += dot(mixt[blk], ga[at])

        @pl.when(i == g.n_t - 1)
        def _():
            zo.sent()
            wa[3] = turned(middle[0:c].astype(BF))
            zscat[3].start()

        go_t = dot(wo_t[...], ga[at], NT).astype(BF).astype(F32)
        mix_t = mixt[blk].astype(F32)
        scaled, dots = [], []
        for h in range(H):
            one_head = go_t[h * HD : (h + 1) * HD] * rinv[blk, h : h + 1, :]
            scaled.append(one_head)
            dots.append(jnp.sum(one_head * mix_t[h * HD : (h + 1) * HD], axis=0, keepdims=True))
        go = jnp.concatenate(scaled, axis=0).T.astype(BF)
        q_blk = q[at]
        for h in range(H):
            gom[h * R : (h + 1) * R] = head_lanes(go, h)
            qm[h * R : (h + 1) * R] = head_lanes(q_blk, h)

        @in_slot(g, n_pic, blk)
        def _(p, index, hi):
            dq = attend_back(g, hi, v, turn, probs[p].at[index], gom, qm, dots, dk, dv).T * HD**-0.5
            q[at] = rotated(dq, cosine[at], -sine[at]).astype(BF)

        pl.when(i == 0)(ag.relay)

        @pl.when(i == 2)
        def _():
            zscat[1].relay(0)
            zscat[1].relay(1)

    @pl.loop(0, g.n_t)
    def _(i):
        at = g.rows(g.leave_at(i))
        kk[at] = rotated(dk[at], cosine[at], -sine[at]).astype(BF)
        v[at] = dv[at].astype(BF)
        partial = dot(q[at], wa[0], NT) + dot(kk[at], wa[1], NT) + dot(v[at], wa[2], NT)

        @pl.when(i < g.n_t - 1)
        def _():
            rs.give(i, partial)

        @pl.when(i == g.n_t - 1)
        def _():
            grad_inputs[...] = partial


    zscat[3].pass_on()
    zscat[1].relay(2)
    zscat[2].relay(0)
    zscat[2].relay(1)
    za.sent()
    for j in range(3):
        wa[j] = dot(rows1[...], qkv[j]).astype(BF)
        zscat[4 + j].start()
    for j in (4, 5, 6):
        zscat[j].meet()
        zscat[j].part(0)
    rs.relay()
    for k in (1, 2):
        for j in (4, 5, 6):
            zscat[j].part(k)
    zscat[2].relay(2)
    zscat[3].relay(0)
    zscat[3].relay(1)
    one, inv = normed(x[...])

    for j, to in enumerate((o_g, o_u, o_d)):
        dmlp[j] = zscat[j].total().T
        store(dmlp.at[j], to)
    for j in (4, 5, 6):
        zscat[j].relay(0)
    zscat[3].relay(2)
    for j, k in ((4, 2), (5, 2), (4, 1), (6, 2), (5, 1)):
        zscat[j].relay(k)
    for i in range(2):
        for rows, back in rs.take(i, grad_inputs):
            grad_inputs[rows] = cot[rows] + normed_back(one[rows], inv[rows], back)
    store(grad_inputs, o_in)
    zscat[6].relay(1)
    dout[...] = zscat[3].total().T
    store(dout, o_o)
    total = err[base + 2]
    for k in range(1, C):
        zc.recv(ez[k - 1], err.at[base + 2 + k], (g.zfrom(k), g.t))
        total = total + err[base + 2 + k]
    stats[...] = (total * (1.0 / g.D) / tokens)[0:1, 0:1]
    store(stats, o_loss)
    for j, to in enumerate((o_q, o_k, o_v)):
        dattn[j] = zscat[4 + j].total()
        store(dattn.at[j], to)
    for copy in stores:
        copy.wait()
    ag.sent()
    for scat in zscat:
        scat.sent()
    tc.sent(few, err.at[0 : len(te)], (g.sib, g.t))
    for group, n in ((gsib, 1), (gz, C - 1), (gec, 1), (gez, C - 1)):
        zc.sent(group, cnt.at[0:n], (g.sib, g.t))
    assert tc.n <= tr.shape[0] and zc.n <= zr.shape[0] and tc.groups <= ts.shape[0] and zc.groups <= zs.shape[0]


def layer(g, n_pic, args):
    S, R, D, c, f, H, C, Dn = g.S, g.R, g.D, g.c, g.f, g.H, g.C, g.Dn
    sds, V = jax.ShapeDtypeStruct, pltpu.VMEM
    shapes = [(R, D), (R, D), (Dn, c), (Dn, c), (Dn, c), (c, Dn), (f, Dn), (f, Dn), (f, Dn), (1, 1)]
    outs = [sds(s, F32) for s in shapes]
    base = 4 if g.square else g.n_t
    scratch = [V((S, D), BF)] * 4 + [
        V((4, D, c), BF), V((3, D, f), BF), V((3, S, c), BF), V((S, c), BF), V((g.n_t, c, R), BF), V((c, S), BF), V((c, D), BF),
        V((g.n_t // 2, S // 2, H * R), BF), V((g.n_t // 2, S, H * R), BF), V((2, S, max(R, c)), F32), V((H * R, c), BF), V((H * R, c), BF), V((3, S, f), BF),
        V((max(R, c), D), F32), V((R, D), F32), V((8, S), jnp.int32), V((S, 128), jnp.int32), V((g.n_t, 8, R), F32),
        V((2 + C, 8, 128), F32), V((base + 2 + C, 8, 128), F32),
    ]
    scratch += scatter_scratch(g)
    m = weight_scatter_scratch(g, 3, f)
    scratch += [m[0], m[2]] + weight_scatter_scratch(g, 4, c)
    scratch += [V((R, D), F32), V((R, D), F32), V((3, Dn, c), F32), V((c, Dn), F32), V((3, f, Dn), F32), V((1, 1), F32)]
    nt = 20 if g.square else 3 * (g.n_t - 1)
    nz = 4 * (2 * C - 1) + 7 * (6 if g.line else C) + 2 * C
    sem = pltpu.SemaphoreType.DMA
    scratch += [sem((3,)), sem((nt,)), sem((15,)), sem((nz,)), sem((11,))]
    whole = pl.BlockSpec(memory_space=pltpu.VMEM)
    specs = [whole] * len(args)
    specs[1] = pl.BlockSpec(memory_space=pl.ANY)
    return pl.pallas_call(
        functools.partial(layer_body, g, n_pic),
        name="layer",
        out_shape=outs,
        in_specs=specs,
        out_specs=[pl.BlockSpec(memory_space=pl.ANY)] * len(outs),
        scratch_shapes=scratch,
        compiler_params=pltpu.CompilerParams(collective_id=1, has_side_effects=True, vmem_limit_bytes=VMEM_BYTES),
    )(*args)


def finish_body(n, *refs):
    parts, outs, bufs, come, go = refs[:n], refs[n : 2 * n], refs[2 * n : 3 * n], refs[3 * n], refs[3 * n + 1]
    loads = [pltpu.make_async_copy(a, b, come.at[k]) for k, (a, b) in enumerate(zip(parts, bufs))]
    stores = [pltpu.make_async_copy(a, b, go.at[k]) for k, (a, b) in enumerate(zip(bufs, outs))]
    for copy in loads:
        copy.start()
    for load, store in zip(loads, stores):
        load.wait()
        store.start()
    for copy in stores:
        copy.wait()


def finish(parts):
    anywhere, n = pl.BlockSpec(memory_space=pl.ANY), len(parts)
    return pl.pallas_call(
        functools.partial(finish_body, n),
        name="finish",
        out_shape=[jax.ShapeDtypeStruct(p.shape, F32) for p in parts],
        in_specs=[anywhere] * n,
        out_specs=[anywhere] * n,
        scratch_shapes=[pltpu.VMEM(p.shape, F32) for p in parts] + [pltpu.SemaphoreType.DMA((n,))] * 2,
    )(*parts)


def per_device(n_dp, n_t, inputs, teacher, valid_mask, documents, picture_starts,
               w_query, w_key, w_value, w_out, w_gate, w_up, w_down):
    R, D = inputs.shape
    c, f = w_query.shape[1], w_gate.shape[1]
    g = Geo(n_dp, n_t, R, D, c, f)
    args = (inputs, teacher, valid_mask, documents, picture_starts, w_query, w_key, w_value, w_out, w_gate.T, w_up.T, w_down)
    parts = layer(g, picture_starts.shape[1], (*args, *rotary(g.S, c)))
    out, *grads, gate, up, down, loss = finish(parts)
    return (out, loss.reshape(()), *grads, gate.T, up.T, down)


def solution(mesh):
    rows, pair = P(("dp", "tensor"), None), P("dp", None)
    cut, across = P("dp", "tensor"), P("tensor", "dp")
    return jax.shard_map(
        functools.partial(per_device, mesh.shape["dp"], mesh.shape["tensor"]),
        mesh=mesh,
        in_specs=(rows, rows, pair, pair, pair, cut, cut, cut, across, cut, cut, across),
        out_specs=(rows, P(), rows, cut, cut, cut, across, cut, cut, across),
        check_vma=False,
    )
```

profile of v0, /device:TPU:0, one launch (start us, length us, event | category | flops | bytes accessed | tf_op | source)
XLA Modules:
  0.0 173.1 jit_solution(2547712763467411288)
XLA Ops:
  0.6 168.4 %layer.1 = (f32[256,1024]{1,0:T(8,128)}, f32[256,1024]{1,0:T(8,128)}, f32[128,256]{1,0:T(8,128)}, f32[128,256]{1,0:T(8,128)}, f32[128,256]{1,0:T(8,128)}, /*inde...) custom-call(f32[256,1024]{1,0:T(8,128)} %x.1, ...), custom_call_target="tpu_custom_call" | custom-call | tf_op jit(solution)/shard_map/layer/pallas_call | solution.py:1003
  169.0 3.9 %finish.1 = (f32[256,1024]{1,0:T(8,128)}, f32[256,1024]{1,0:T(8,128)}, f32[128,256]{1,0:T(8,128)}, f32[128,256]{1,0:T(8,128)}, f32[128,256]{1,0:T(8,128)}, /*ind...) custom-call(f32[256,1024]{1,0:T(8,128)} %get-tuple-element.30.refs_0_, ...), custom_call_target="tpu_custom_call" | custom-call | tf_op jit(solution)/shard_map/finish/pallas_call | solution.py:1029
where the time goes:
time: 175 us; the launch traced here: 173 us
  Pallas kernels  172 us (98%)
    pallas_call x1, Pallas kernels, layer(): pl.pallas_call(functools.partial(layer_body, g, n_pic), name='layer', out...  168 us
    pallas_call x1, Pallas kernels, finish(): pl.pallas_call(functools.partial(finish_body, n), name='finish', out_shap...  3.86 us

commit v1 on v0

--- a/solution.py
+++ b/solution.py
@@ -33,7 +33,7 @@
 def turned(a):
     n = a.shape[1]
     step = min(n, 256)
-    parts = [dot(eye(step), a[:, k : k + step], NT).astype(BF) for k in range(0, n, step)]
+    parts = [dot(eye(min(step, n - k)), a[:, k : k + step], NT).astype(BF) for k in range(0, n, step)]
     return parts[0] if len(parts) == 1 else jnp.concatenate(parts, axis=0)
 
 
@@ -381,8 +381,8 @@
 
 
 class WeightScatter:
-    def __init__(self, geo, comm, src, bufs):
-        self.g, self.comm, self.src = geo, comm, src
+    def __init__(self, geo, comm, block, most, bufs):
+        self.g, self.comm, self.block, self.most = geo, comm, block, most
         self.sib_in, self.out, self.fin = bufs
         g = geo
         self.group = comm.group()
@@ -394,11 +394,10 @@
     def start(self):
         g, comm = self.g, self.comm
         for j in range(g.C):
-            block = self.src.at[g.wrows(2 * j + 1 - g.core)]
-            comm.send(self.group, self.sc, block, self.sib_in.at[j], (g.sib, g.t))
+            comm.send(self.group, self.sc, self.block(2 * j + 1 - g.core), self.sib_in.at[j], (g.sib, g.t))
 
     def _sum(self, chip):
-        return self.src[self.g.wrows(2 * chip + self.g.core)].astype(F32) + self.sib_in[chip].astype(F32)
+        return self.block(2 * chip + self.g.core)[...].astype(F32) + self.sib_in[chip].astype(F32)
 
     def meet(self):
         g, comm = self.g, self.comm
@@ -442,12 +441,11 @@
         comm.send(self.group, self.sz[goes], self.out[b], self.fin.at[goes], to, when=middle)
 
     def sent(self):
-        g = self.g
-        self.comm.sent(self.group, self.src.at[0 : (2 * g.C - 1) * g.Dn], (g.sib, g.t))
+        self.comm.sent(self.group, self.most, (self.g.sib, self.g.t))
 
     def total(self):
         g, comm = self.g, self.comm
-        mine = self.src[g.wrows(g.d)].astype(F32) + self.sib_in[g.chip].astype(F32)
+        mine = self.block(g.d)[...].astype(F32) + self.sib_in[g.chip].astype(F32)
         if not g.line:
             for k in range(1, g.C):
                 comm.recv(self.sz[k - 1], self.fin.at[k - 1], (g.zfrom(k), g.t))
@@ -462,9 +460,9 @@
         return mine + jnp.where(self.end, at_end, between)
 
 
-def weight_scatter_scratch(g, n, w):
+def weight_scatter_scratch(g, n, rows, w):
     steps = 5 if g.line else g.C - 1
-    return [pltpu.VMEM((n, g.C, g.Dn, w), BF), pltpu.VMEM((n, g.C - 1, g.Dn, w), BF), pltpu.VMEM((n, steps, g.Dn, w), BF)]
+    return [pltpu.VMEM((n, g.C, rows, w), BF), pltpu.VMEM((n, g.C - 1, rows, w), BF), pltpu.VMEM((n, steps, rows, w), BF)]
 
 
 def rotated(v, cosine, sine):
@@ -569,6 +567,10 @@
     return (jnp.asarray(np.tile(cosine, (1, reps)), F32), jnp.asarray(np.tile(sine, (1, reps)), F32))
 
 
+def in_lanes(g):
+    return g.Dn % 128 == 0 and g.f <= g.S and (g.C - 1) * g.Dn <= g.f and 2 * g.Dn <= max(g.R, g.c)
+
+
 def in_slot(g, n_pic, blk):
     per = g.n_t // n_pic
 
@@ -584,7 +586,7 @@
                rows1, rows2, gm, ga, wa, wm, qkv, mixed, mixt, turn, wo_t, probs0, probs1, acc2, qm, gom, mids, middle, cot,
                qinfo, kinfo, rinv, cnt, err,
                part, into, out, fin,
-               sib_m, fin_m, sib_a, out_a, fin_a, output, grad_inputs, dattn, dout, dmlp, stats,
+               hidden_t, down, sib_d, spare_d, fin_d, sib_m, fin_m, sib_a, out_a, fin_a, output, grad_inputs, dattn, dout, spare_m, stats,
                ts, tr, zs, zr, local):
     g.place()
     g.greet()
@@ -600,7 +602,14 @@
     q, kk, v = qkv.at[0], qkv.at[1], qkv.at[2]
     probs = (probs0, probs1)
     bias, dk, dv = acc2.at[:, :, :R], acc2.at[0, :, :c], acc2.at[1, :, :c]
+    packed = in_lanes(g)
     stores = []
+
+    def out_d(k):
+        return mids.at[0, 0 : g.f, k * Dn : (k + 1) * Dn] if packed else spare_d.at[k]
+
+    def total_m(j):
+        return acc2.at[j % 2, 0 : g.f, j // 2 * Dn : (j // 2 + 1) * Dn] if packed else spare_m.at[j]
 
     def store(buf, to):
         copy = pltpu.make_async_copy(buf, to, local.at[1 + len(stores)])
@@ -746,6 +755,7 @@
     output[...] = middle[0:R] + dot(mids[0, g.rows(g.t)], wm[2], NT)
     wo_t[...] = turned(wa[3])
     rs.relay()
+    hidden_t[...] = turned(mids[0])
 
     get_teacher.wait()
     tokens = cnt[2]
@@ -776,6 +786,9 @@
         for k, peer in enumerate(g.to):
             tc.send(few, te[k], err.at[0], err.at[1 + k], (g.d, peer))
 
+    zscat = [WeightScatter(g, zc, lambda d: down.at[d], down.at[0 : 2 * C - 1],
+                           (sib_d.at[0], [out_d(k) for k in range(C - 1)], fin_d.at[0]))]
+
     @pl.loop(0, g.n_t)
     def _(i):
         for k in range(1, g.n_t):
@@ -795,27 +808,27 @@
         def _():
             rs.give(g.far_lead(i), dot(mids[1, at], wm[0], NT) + dot(mids[2, at], wm[1], NT))
 
+    wide = max(256, Dn)
+
+    @pl.loop(0, g.D // wide)
+    def _(k):
+        some = dot(hidden_t[...], gm[:, pl.ds(pl.multiple_of(k * wide, wide), wide)]).astype(BF)
+        for n in range(wide // Dn):
+            down[k * (wide // Dn) + n] = some[:, n * Dn : (n + 1) * Dn]
+
+    zscat[0].start()
+    rs.relay()
     at = g.rows(g.t)
     grad_inputs[...] = dot(mids[1, at], wm[0], NT) + dot(mids[2, at], wm[1], NT)
+    zscat[0].pass_on()
     zg.sent()
     zd.sent()
-    wm[0] = dot(rows2[...], mids[1]).astype(BF)
-
-    zscat = []
-
-    def start_mlp(j, used):
-        spare = [mids.at[used, k * Dn : (k + 1) * Dn] for k in range(C - 1)]
-        zscat.append(WeightScatter(g, zc, wm.at[j], (sib_m.at[j], spare, fin_m.at[j])))
+    for j in range(2):
+        wm[j] = dot(rows2[...], mids[1 + j]).astype(BF)
+        spare = [mids.at[1 + j, k * Dn : (k + 1) * Dn] for k in range(C - 1)]
+        zscat.append(WeightScatter(g, zc, lambda d, j=j: wm.at[j, g.wrows(d)], wm.at[j, 0 : (2 * C - 1) * Dn],
+                                   (sib_m.at[j], spare, fin_m.at[j])))
         zscat[-1].start()
-
-    start_mlp(0, 1)
-    rs.relay()
-    zscat[0].pass_on()
-    wm[1] = dot(rows2[...], mids[2]).astype(BF)
-    start_mlp(1, 2)
-    for k in range(0, g.D, 256):
-        wm[2, k : k + 256] = dot(turned(gm[:, k : k + 256]), mids[0]).astype(BF)
-    start_mlp(2, 0)
     zscat[1].pass_on()
     two, inv = normed(middle[0:R])
     ag.sent()
@@ -829,7 +842,8 @@
 
     for j in (3, 0, 1, 2):
         spare = [out_a.at[j, k] for k in range(C - 1)]
-        zscat.append(WeightScatter(g, zc, wa.at[j], (sib_a.at[j], spare, fin_a.at[j])))
+        zscat.append(WeightScatter(g, zc, lambda d, j=j: wa.at[j, g.wrows(d)], wa.at[j, 0 : (2 * C - 1) * Dn],
+                                   (sib_a.at[j], spare, fin_a.at[j])))
 
     rs = scatter()
     zscat[2].pass_on()
@@ -942,9 +956,9 @@
     zscat[3].relay(1)
     one, inv = normed(x[...])
 
-    for j, to in enumerate((o_g, o_u, o_d)):
-        dmlp[j] = zscat[j].total().T
-        store(dmlp.at[j], to)
+    for j, to in enumerate((o_d, o_g, o_u)):
+        total_m(j)[...] = zscat[j].total().T if j else zscat[j].total()
+        store(total_m(j), to)
     for j in (4, 5, 6):
         zscat[j].relay(0)
     zscat[3].relay(2)
@@ -955,8 +969,9 @@
             grad_inputs[rows] = cot[rows] + normed_back(one[rows], inv[rows], back)
     store(grad_inputs, o_in)
     zscat[6].relay(1)
-    dout[...] = zscat[3].total().T
-    store(dout, o_o)
+    dout_at = acc2.at[1, 0:c, Dn : 2 * Dn] if packed else dout
+    dout_at[...] = zscat[3].total().T
+    store(dout_at, o_o)
     total = err[base + 2]
     for k in range(1, C):
         zc.recv(ez[k - 1], err.at[base + 2 + k], (g.zfrom(k), g.t))
@@ -990,9 +1005,12 @@
         V((2 + C, 8, 128), F32), V((base + 2 + C, 8, 128), F32),
     ]
     scratch += scatter_scratch(g)
-    m = weight_scatter_scratch(g, 3, f)
-    scratch += [m[0], m[2]] + weight_scatter_scratch(g, 4, c)
-    scratch += [V((R, D), F32), V((R, D), F32), V((3, Dn, c), F32), V((c, Dn), F32), V((3, f, Dn), F32), V((1, 1), F32)]
+    m = weight_scatter_scratch(g, 2, Dn, f)
+    d = weight_scatter_scratch(g, 1, f, Dn)
+    few = V((1, 16, 128), BF)
+    scratch += [V((f, S), BF), V((g.n_dp, f, Dn), BF), d[0], few if in_lanes(g) else V((C - 1, f, Dn), BF), d[2]]
+    scratch += [m[0], m[2]] + weight_scatter_scratch(g, 4, Dn, c)
+    scratch += [V((R, D), F32), V((R, D), F32), V((3, Dn, c), F32), few if in_lanes(g) else V((c, Dn), F32), few if in_lanes(g) else V((3, f, Dn), F32), V((1, 1), F32)]
     nt = 20 if g.square else 3 * (g.n_t - 1)
     nz = 4 * (2 * C - 1) + 7 * (6 if g.line else C) + 2 * C
     sem = pltpu.SemaphoreType.DMA

time: 175 us -> 174 us (level); the launches traced: 173 us -> 174 us
  no operation moved by 1% of the time
where the time goes in v1:
time: 174 us
  Pallas kernels  173 us (99%)
    pallas_call x1, Pallas kernels, layer(): pl.pallas_call(functools.partial(layer_body, g, n_pic), name='layer', out...  169 us
    pallas_call x1, Pallas kernels, finish(): pl.pallas_call(functools.partial(finish_body, n), name='finish', out_shap...  3.86 us

profile of v1, /device:TPU:0, one launch (start us, length us, event | category | flops | bytes accessed | tf_op | source)
XLA Modules:
  0.0 174.0 jit_solution(17252598459893943063)
XLA Ops:
  0.6 169.3 %layer.1 = (f32[256,1024]{1,0:T(8,128)}, f32[256,1024]{1,0:T(8,128)}, f32[128,256]{1,0:T(8,128)}, f32[128,256]{1,0:T(8,128)}, f32[128,256]{1,0:T(8,128)}, /*inde...) custom-call(f32[256,1024]{1,0:T(8,128)} %x.1, ...), custom_call_target="tpu_custom_call" | custom-call | tf_op jit(solution)/shard_map/layer/pallas_call | solution.py:1021
  170.0 3.9 %finish.1 = (f32[256,1024]{1,0:T(8,128)}, f32[256,1024]{1,0:T(8,128)}, f32[128,256]{1,0:T(8,128)}, f32[128,256]{1,0:T(8,128)}, f32[128,256]{1,0:T(8,128)}, /*ind...) custom-call(f32[256,1024]{1,0:T(8,128)} %get-tuple-element.30.refs_0_, ...), custom_call_target="tpu_custom_call" | custom-call | tf_op jit(solution)/shard_map/finish/pallas_call | solution.py:1047

commit v2 on v1

--- a/solution.py
+++ b/solution.py
@@ -581,13 +581,13 @@
     return run
 
 
-def layer_body(g, n_pic, x, teacher, valid_mask, documents, starts, wq, wk, wv, wo, wg, wu, wd, cosine, sine,
+def layer_body(g, n_pic, x, teacher, valid_mask, documents, starts, wq, wk, wv, wo_in, wg_in, wu_in, wd_in, cosine_in, sine_in,
                o_out, o_in, o_q, o_k, o_v, o_o, o_g, o_u, o_d, o_loss,
                rows1, rows2, gm, ga, wa, wm, qkv, mixed, mixt, turn, wo_t, probs0, probs1, acc2, qm, gom, mids, middle, cot,
                qinfo, kinfo, rinv, cnt, err,
                part, into, out, fin,
                hidden_t, down, sib_d, spare_d, fin_d, sib_m, fin_m, sib_a, out_a, fin_a, output, grad_inputs, dattn, dout, spare_m, stats,
-               ts, tr, zs, zr, local):
+               wo, wg, wu, wd, cosine, sine, ts, tr, zs, zr, local):
     g.place()
     g.greet()
     R, S, c, H, C, Dn = g.R, g.S, g.c, g.H, g.C, g.Dn
@@ -616,15 +616,21 @@
         copy.start()
         stores.append(copy)
 
-    get_teacher = pltpu.make_async_copy(teacher, cot, local.at[0])
-    get_teacher.start()
+    def load(k, source, into):
+        copy = pltpu.make_async_copy(source, into, local.at[k])
+        copy.start()
+        return copy
+
+    block = g.wrows(g.d)
+    get_qkv = [load(11 + j, w, wa.at[j, block]) for j, w in enumerate((wq, wk, wv))]
+    get_rest = [load(14, wo_in, wo), load(15, wg_in, wg), load(16, wu_in, wu), load(17, wd_in, wd)]
+    get_tables = [load(18, cosine_in, cosine), load(19, sine_in, sine)]
+    get_teacher = load(0, teacher, cot)
 
     one, _ = normed(x[...])
     rows1[g.rows(g.t)] = one.astype(BF)
-    block = g.wrows(g.d)
-    wa[0, block] = wq[...]
-    wa[1, block] = wk[...]
-    wa[2, block] = wv[...]
+    for copy in get_qkv:
+        copy.wait()
     g.meet()
     ag = gather(rows1)
     ag.begin(0)
@@ -632,6 +638,8 @@
     za, zo = WeightGather(g, zc, wa, 0, 3), WeightGather(g, zc, wa, 3, 1)
     zg, zd = WeightGather(g, zc, wm, 0, 2), WeightGather(g, zc, wm, 2, 1)
     za.far()
+    for copy in get_rest + get_tables:
+        copy.wait()
     wa[3, block] = turned(wo[...])
     zo.far()
     za.near()
@@ -1014,10 +1022,12 @@
     nt = 20 if g.square else 3 * (g.n_t - 1)
     nz = 4 * (2 * C - 1) + 7 * (6 if g.line else C) + 2 * C
     sem = pltpu.SemaphoreType.DMA
-    scratch += [sem((3,)), sem((nt,)), sem((15,)), sem((nz,)), sem((11,))]
+    scratch += [V(a.shape, a.dtype) for a in args[8:14]]
+    scratch += [sem((3,)), sem((nt,)), sem((15,)), sem((nz,)), sem((20,))]
     whole = pl.BlockSpec(memory_space=pltpu.VMEM)
     specs = [whole] * len(args)
-    specs[1] = pl.BlockSpec(memory_space=pl.ANY)
+    for k in (1, *range(5, 14)):
+        specs[k] = pl.BlockSpec(memory_space=pl.ANY)
     return pl.pallas_call(
         functools.partial(layer_body, g, n_pic),
         name="layer",

time: 174 us -> 174 us (level)
  no operation moved by 1% of the time
where the time goes in v2:
time: 174 us; the launch traced here: 173 us
  Pallas kernels  173 us (99%)
    pallas_call x1, Pallas kernels, layer(): pl.pallas_call(functools.partial(layer_body, g, n_pic), name='layer', out...  169 us
    pallas_call x1, Pallas kernels, finish(): pl.pallas_call(functools.partial(finish_body, n), name='finish', out_shap...  3.86 us

profile of v2, /device:TPU:0, one launch (start us, length us, event | category | flops | bytes accessed | tf_op | source)
XLA Modules:
  0.0 173.5 jit_solution(12490684212461498036)
XLA Ops:
  0.6 168.7 %layer.1 = (f32[256,1024]{1,0:T(8,128)}, f32[256,1024]{1,0:T(8,128)}, f32[128,256]{1,0:T(8,128)}, f32[128,256]{1,0:T(8,128)}, f32[128,256]{1,0:T(8,128)}, /*inde...) custom-call(f32[256,1024]{1,0:T(8,128)} %x.1, ...), custom_call_target="tpu_custom_call" | custom-call | tf_op jit(solution)/shard_map/layer/pallas_call | solution.py:1031
  169.4 3.9 %finish.1 = (f32[256,1024]{1,0:T(8,128)}, f32[256,1024]{1,0:T(8,128)}, f32[128,256]{1,0:T(8,128)}, f32[128,256]{1,0:T(8,128)}, f32[128,256]{1,0:T(8,128)}, /*ind...) custom-call(f32[256,1024]{1,0:T(8,128)} %get-tuple-element.30.refs_0_, ...), custom_call_target="tpu_custom_call" | custom-call | tf_op jit(solution)/shard_map/finish/pallas_call | solution.py:1057

commit v3 on v2

--- a/solution.py
+++ b/solution.py
@@ -826,9 +826,9 @@
 
     zscat[0].start()
     rs.relay()
+    zscat[0].pass_on()
     at = g.rows(g.t)
     grad_inputs[...] = dot(mids[1, at], wm[0], NT) + dot(mids[2, at], wm[1], NT)
-    zscat[0].pass_on()
     zg.sent()
     zd.sent()
     for j in range(2):

time: 174 us -> 173 us (level)
  no operation moved by 1% of the time
where the time goes in v3:
time: 173 us; the launch traced here: 172 us
  Pallas kernels  172 us (99%)
    pallas_call x1, Pallas kernels, layer(): pl.pallas_call(functools.partial(layer_body, g, n_pic), name='layer', out...  168 us
    pallas_call x1, Pallas kernels, finish(): pl.pallas_call(functools.partial(finish_body, n), name='finish', out_shap...  3.86 us

profile of v3, /device:TPU:0, one launch (start us, length us, event | category | flops | bytes accessed | tf_op | source)
XLA Modules:
  0.0 172.4 jit_solution(10198972178489099323)
XLA Ops:
  0.6 167.7 %layer.1 = (f32[256,1024]{1,0:T(8,128)}, f32[256,1024]{1,0:T(8,128)}, f32[128,256]{1,0:T(8,128)}, f32[128,256]{1,0:T(8,128)}, f32[128,256]{1,0:T(8,128)}, /*inde...) custom-call(f32[256,1024]{1,0:T(8,128)} %x.1, ...), custom_call_target="tpu_custom_call" | custom-call | tf_op jit(solution)/shard_map/layer/pallas_call | solution.py:1031
  168.3 3.9 %finish.1 = (f32[256,1024]{1,0:T(8,128)}, f32[256,1024]{1,0:T(8,128)}, f32[128,256]{1,0:T(8,128)}, f32[128,256]{1,0:T(8,128)}, f32[128,256]{1,0:T(8,128)}, /*ind...) custom-call(f32[256,1024]{1,0:T(8,128)} %get-tuple-element.30.refs_0_, ...), custom_call_target="tpu_custom_call" | custom-call | tf_op jit(solution)/shard_map/finish/pallas_call | solution.py:1057
